TPU v7x, 32 devices: a whole 2x2x4 slice. The times are simulated.
32 devices in a mesh: dp: 8 (over y, x, core), tensor: 4 (over z).
Axes of the slice: x: 2, y: 2, z: 4, core: 2. Of those that a mesh axis runs over, the one named last changes fastest.
Arguments:
- activations: bfloat16 [8192, 2560], P('dp'), may hold values from -16 to 16
- weight: bfloat16 [2560, 5120], P('dp', 'tensor'), may hold values from -0.125 to 0.125
- target: bfloat16 [8192, 5120], P('dp', 'tensor'), may hold values from -6 to 6
- start_vector: float32 [2560, 5120], P('dp', 'tensor'), may hold values from -22.9 to 22.9
- stored: float32 [4, 2560, 5120], P(None, 'dp', 'tensor'), may hold values from -6.8 to 6.8
Outputs:
- krylov: float32 [2, 2560, 5120], P(None, 'dp', 'tensor')
- coef_first: float32 [6], replicated
- coef_second: float32 [7], replicated
- projections: float32 [16, 7], P('dp')
All inputs are finite; a program needn't handle non-finite values.
Results may differ from a plain program's by a relative error of at most 0.0052.
Values may be sent and summed in bfloat16 or wider, within the bound.
A program may use at most 320 MiB of HBM per device.

v0:
```python
import math

import jax
import jax.numpy as jnp
from jax import lax
from jax.sharding import PartitionSpec as P

A = 2560
D = 5120
EX_DEV = 2
KS = 4
ITERS = 2
TOK_EX = 512


def local_products(vectors, imaged):
    return jnp.sum(vectors * imaged[None], axis=(1, 2))


def combine(coeffs, vectors):
    return jnp.sum(coeffs[:, None, None] * vectors, axis=0)


def shards(activations, weight, target, start_vector, stored):
    total_rows = activations.shape[0] * lax.axis_size("dp")
    nparam = float(A * D)
    col_width = weight.shape[1]
    hidden = jnp.dot(
        activations,
        lax.all_gather(weight, "dp", axis=0, tiled=True),
        preferred_element_type=jnp.float32,
    )
    residual_tanh = jnp.tanh(hidden - target.astype(jnp.float32))
    curvature = (1.0 - residual_tanh * residual_tanh) / total_rows
    kept_dirs = []
    columns_out = []
    square_sum = lax.psum(jnp.sum(start_vector * start_vector), ("dp", "tensor"))
    vectors = jnp.concatenate(
        [stored, (start_vector / jnp.sqrt(square_sum / nparam))[None]], axis=0
    )
    for iteration in range(ITERS):
        direction = vectors[-1].astype(jnp.bfloat16)
        gathered_dir = lax.all_gather(direction, "dp", axis=0, tiled=True)
        mapped = jnp.dot(activations, gathered_dir, preferred_element_type=jnp.float32)
        scaled = (curvature * mapped).astype(jnp.bfloat16)
        imaged, gathered_dir = (
            lax.psum_scatter(
                lax.dot_general(
                    activations,
                    scaled,
                    (((0,), (0,)), ((), ())),
                    preferred_element_type=jnp.float32,
                ),
                "dp",
                scatter_dimension=0,
                tiled=True,
            ),
            gathered_dir,
        )
        kept_dirs.append(gathered_dir)
        first_coef = lax.psum(local_products(vectors, imaged), ("dp", "tensor")) / nparam
        remainder = imaged - combine(first_coef, vectors)
        second = lax.psum(local_products(vectors, remainder), ("dp", "tensor")) / nparam
        remainder = remainder - combine(second, vectors)
        length_norm = jnp.sqrt(lax.psum(jnp.sum(remainder * remainder), ("dp", "tensor")) / nparam)
        columns_out.append(jnp.concatenate([first_coef + second, length_norm[None]]))
        vectors = jnp.concatenate([vectors, (remainder / length_norm)[None]], axis=0)
    signs = residual_tanh.astype(jnp.bfloat16)
    example_rows = activations.reshape(EX_DEV, TOK_EX, activations.shape[1])
    example_signs = signs.reshape(EX_DEV, TOK_EX, col_width)
    grads = jnp.einsum(
        "eta,etd->ead", example_rows, example_signs, preferred_element_type=jnp.float32
    ).astype(jnp.bfloat16)
    local_table = vectors.astype(jnp.bfloat16)
    extra_rows = jnp.concatenate([local_table[:KS], local_table[-1:]], axis=0)
    full_extra = lax.all_gather(extra_rows, "dp", axis=1, tiled=True)
    basis_table = jnp.concatenate([full_extra[:KS], jnp.stack(kept_dirs), full_extra[-1:]], axis=0)
    partial_value = jnp.einsum(
        "ead,kad->ek", grads, basis_table, preferred_element_type=jnp.float32
    )
    projections = lax.psum(partial_value, "tensor")
    projections = projections / math.sqrt(float(TOK_EX) * nparam)
    krylov = vectors[KS + 1 :]
    return (krylov, columns_out[0], columns_out[1], projections)


def solution(mesh):
    in_specs = (
        P("dp", None),
        P("dp", "tensor"),
        P("dp", "tensor"),
        P("dp", "tensor"),
        P(None, "dp", "tensor"),
    )
    out_specs = (P(None, "dp", "tensor"), P(), P(), P("dp", None))
    return jax.shard_map(shards, mesh=mesh, in_specs=in_specs, out_specs=out_specs, check_vma=False)
```

profile of v0, /device:TPU:0, one launch (start us, length us, event | category | flops | bytes accessed | tf_op | source)
XLA Modules:
  0.0 1123.8 jit_solution(2617764496018569613)
XLA Ops:
  7.9 2.5 multiply_reduce_fusion.10
  10.4 42.6 %psum.56 = f32[]{:T(128)} all-reduce(f32[]{:T(128)} %multiply_reduce_fusion.10), channel_id=1, replica_groups=mesh['dp'=8,'tensor'=4] {'dp','tensor'}, use_global_device_ids=true, to_apply=%region_1.0 | all-reduce | flops 1 | bytes 8 | tf_op jit(solution)/shard_map/psum | solution.py:37
  53.7 2.5 fusion.14
  56.3 3.9 all-gather.5.cloned.1.call-done
  60.1 13.1 %fusion.22 = (bf16[1024,1280]{1,0:T(8,128)(2,1)}, f32[1024,1280]{1,0:T(8,128)}) fusion(bf16[1024,1280]{1,0:T(8,128)(2,1)} %param.7, bf16[1024,2560]{1,0:T(8,128)(2,1)} %param.5, bf16[2560,1280]{1,0:T(8,128)(2,1)} %all-gather.5.cloned.1.call-done), kind=kOutput, calls=%fused_computation.52 | convolution fusion | flops 6714818560 | bytes 22282240 | tf_op jit(solution)/shard_map/dot_general | solution.py:28
  73.2 35.9 %all-gather.7.cloned.1.call-done = bf16[2560,1280]{1,0:T(8,128)(2,1)} async-done(((bf16[320,1280]{1,0:T(8,128)(2,1)}), bf16[2560,1280]{1,0:T(8,128)(2,1)}) %all-gather.7.cloned.1.call-update) | async-done | bytes 6553616 | tf_op jit(solution)/shard_map/all_gather | solution.py:43
  109.2 11.6 %fusion.10 = bf16[1024,1280]{1,0:T(8,128)(2,1)S(1)} fusion(f32[1024,1280]{1,0:T(8,128)} %get-tuple-element.27, bf16[1024,2560]{1,0:T(8,128)(2,1)} %param.5, bf16[2560,1280]{1,0:T(8,128)(2,1)} %all-gather.7.cloned.1.call-done), kind=kOutput, calls=%fused_computation.25 | convolution fusion | flops 6717440000 | bytes 19660800 | tf_op jit(solution)/shard_map/dot_general | solution.py:44
  120.7 12.5 %convolution_bitcast_fusion.1 = f32[2560,1280]{0,1:T(8,128)} fusion(bf16[1024,1280]{1,0:T(8,128)(2,1)S(1)} %fusion.10, bf16[1024,2560]{1,0:T(8,128)(2,1)} %param.5), kind=kOutput, calls=%fused_computation.11 | convolution fusion | flops 6710886400 | bytes 20971520 | tf_op jit(solution)/shard_map/dot_general | solution.py:48
  133.3 14.0 %copy.54 = f32[2560,1280]{1,0:T(8,128)} copy(f32[2560,1280]{0,1:T(8,128)} %convolution_bitcast_fusion.1) | data formatting | bytes 26214400
  147.3 95.3 %reduce-scatter.7.cloned.1.call-done = f32[320,1280]{1,0:T(8,128)} async-done(((f32[2560,1280]{1,0:T(8,128)}), f32[320,1280]{1,0:T(8,128)}) %reduce-scatter.7.cloned.1.call-update) | async-done | bytes 1638416 | tf_op jit(solution)/shard_map/reduce_scatter | solution.py:47
  242.6 4.0 multiply_reduce_fusion.7
  246.5 39.5 %psum.57 = f32[5]{0:T(128)S(1)} all-reduce(f32[5]{0:T(128)S(1)} %multiply_reduce_fusion.7), channel_id=1, replica_groups=mesh['dp'=8,'tensor'=4] {'dp','tensor'}, use_global_device_ids=true, to_apply=%region_4.0 | all-reduce | flops 5 | bytes 40 | tf_op jit(solution)/shard_map/psum | solution.py:61
  286.1 3.9 multiply_reduce_fusion.6
  291.4 1.4 multiply_reduce_fusion.5
  292.7 40.7 %psum.58 = f32[5]{0:T(128)S(1)} all-reduce(f32[5]{0:T(128)S(1)} %multiply_reduce_fusion.5), channel_id=1, replica_groups=mesh['dp'=8,'tensor'=4] {'dp','tensor'}, use_global_device_ids=true, to_apply=%region_7.0 | all-reduce | flops 5 | bytes 40 | tf_op jit(solution)/shard_map/psum | solution.py:63
  333.5 3.7 multiply_reduce_fusion.4
  337.2 1.0 multiply_reduce_fusion.9
  338.2 39.4 %psum.59 = f32[]{:T(128)} all-reduce(f32[]{:T(128)} %get-tuple-element.16), channel_id=1, replica_groups=mesh['dp'=8,'tensor'=4] {'dp','tensor'}, use_global_device_ids=true, to_apply=%region_10.0 | all-reduce | flops 1 | bytes 8 | tf_op jit(solution)/shard_map/psum | solution.py:65
  378.4 1.6 fusion.17
  380.0 47.5 %all-gather.9.cloned.1.call-done = bf16[2560,1280]{1,0:T(8,128)(2,1)} async-done(((bf16[320,1280]{1,0:T(8,128)(2,1)}), bf16[2560,1280]{1,0:T(8,128)(2,1)}) %all-gather.9.cloned.1.call-update) | async-done | bytes 6553616 | tf_op jit(solution)/shard_map/all_gather | solution.py:43
  427.5 11.6 %fusion.9 = bf16[1024,1280]{1,0:T(8,128)(2,1)S(1)} fusion(f32[1024,1280]{1,0:T(8,128)} %get-tuple-element.27, bf16[1024,2560]{1,0:T(8,128)(2,1)} %param.5, bf16[2560,1280]{1,0:T(8,128)(2,1)} %all-gather.9.cloned.1.call-done), kind=kOutput, calls=%fused_computation.23 | convolution fusion | flops 6717440000 | bytes 19660800 | tf_op jit(solution)/shard_map/dot_general | solution.py:44
  439.1 12.5 %convolution_bitcast_fusion = f32[2560,1280]{0,1:T(8,128)} fusion(bf16[1024,1280]{1,0:T(8,128)(2,1)S(1)} %fusion.9, bf16[1024,2560]{1,0:T(8,128)(2,1)} %param.5), kind=kOutput, calls=%fused_computation.10 | convolution fusion | flops 6710886400 | bytes 20971520 | tf_op jit(solution)/shard_map/dot_general | solution.py:48
  451.6 14.0 %copy.56 = f32[2560,1280]{1,0:T(8,128)} copy(f32[2560,1280]{0,1:T(8,128)} %convolution_bitcast_fusion) | data formatting | bytes 26214400
  465.7 95.3 %reduce-scatter.9.cloned.1.call-done = f32[320,1280]{1,0:T(8,128)} async-done(((f32[2560,1280]{1,0:T(8,128)}), f32[320,1280]{1,0:T(8,128)}) %reduce-scatter.9.cloned.1.call-update) | async-done | bytes 1638416 | tf_op jit(solution)/shard_map/reduce_scatter | solution.py:47
  560.9 5.1 multiply_reduce_fusion.3
  566.0 50.2 %psum.60 = f32[6]{0:T(128)S(1)} all-reduce(f32[6]{0:T(128)S(1)} %multiply_reduce_fusion.3), channel_id=1, replica_groups=mesh['dp'=8,'tensor'=4] {'dp','tensor'}, use_global_device_ids=true, to_apply=%region_13.0 | all-reduce | flops 6 | bytes 48 | tf_op jit(solution)/shard_map/psum | solution.py:61
  616.2 4.6 multiply_reduce_fusion.2
  621.1 1.1 copy-done.4
  623.6 1.3 multiply_reduce_fusion.1
  624.9 2.0 slice.14
  626.9 40.7 %psum.61 = f32[6]{0:T(128)S(1)} all-reduce(f32[6]{0:T(128)S(1)} %multiply_reduce_fusion.1), channel_id=1, replica_groups=mesh['dp'=8,'tensor'=4] {'dp','tensor'}, use_global_device_ids=true, to_apply=%region_16.0 | all-reduce | flops 6 | bytes 48 | tf_op jit(solution)/shard_map/psum | solution.py:63
  667.6 4.5 multiply_reduce_fusion
  672.2 2.1 multiply_reduce_fusion.8
  674.3 39.4 %psum.62 = f32[]{:T(128)} all-reduce(f32[]{:T(128)} %get-tuple-element.14), channel_id=1, replica_groups=mesh['dp'=8,'tensor'=4] {'dp','tensor'}, use_global_device_ids=true, to_apply=%region_19.0 | all-reduce | flops 1 | bytes 8 | tf_op jit(solution)/shard_map/psum | solution.py:65
  714.5 2.8 fusion.21
  717.3 2.3 pad_maximum_fusion.2
  719.6 13.7 %fusion.8 = bf16[2,2560,1280]{1,2,0:T(8,128)(2,1)} fusion(bf16[2,512,1280]{2,1,0:T(8,128)(2,1)} %bitcast.53, bf16[2,512,2560]{2,1,0:T(8,128)(2,1)} %bitcast.52), kind=kOutput, calls=%fused_computation.9 | convolution fusion | flops 6717440000 | bytes 20971520 | tf_op jit(solution)/shard_map/eta,etd->ead/dot_general | solution.py:71
  733.2 32.7 %copy.50 = bf16[2,2560,1280]{2,0,1:T(2,128)(2,1)} copy(bf16[2,2560,1280]{1,2,0:T(8,128)(2,1)} %fusion.8) | data formatting | bytes 26214400 | tf_op jit(solution)/shard_map/convert_element_type | solution.py:73
  765.9 12.6 %copy.48 = bf16[1,2560,1280]{2,0,1:T(2,128)(2,1)} copy(bf16[1,2560,1280]{2,1,0:T(8,128)(2,1)} %bitcast.50) | data formatting | bytes 13107200 | tf_op jit(solution)/shard_map/stack | solution.py:77
  779.1 12.8 %copy.49 = bf16[1,2560,1280]{2,0,1:T(2,128)(2,1)} copy(bf16[1,2560,1280]{2,1,0:T(8,128)(2,1)} %bitcast.51) | data formatting | bytes 13107200 | tf_op jit(solution)/shard_map/stack | solution.py:77
  792.5 1.9 pad_maximum_fusion.3
  794.5 83.5 %all-gather.11.cloned.1.call-done = bf16[5,2560,1280]{2,1,0:T(8,128)(2,1)} async-done(((bf16[5,320,1280]{2,1,0:T(8,128)(2,1)}), bf16[5,2560,1280]{2,1,0:T(8,128)(2,1)}) %all-gather.11.cloned.1.call-update) | async-done | bytes 32768016 | tf_op jit(solution)/shard_map/all_gather | solution.py:76
  877.9 18.1 %slice.18 = bf16[4,2560,1280]{2,1,0:T(8,128)(2,1)} slice(bf16[5,2560,1280]{2,1,0:T(8,128)(2,1)} %all-gather.11.cloned.1.call-done), slice={[0:4], [0:2560], [0:1280]} | slice | bytes 52428800 | tf_op jit(solution)/shard_map/slice | solution.py:77
  896.1 33.6 %copy.58 = bf16[4,2560,1280]{2,0,1:T(4,128)(2,1)} copy(bf16[4,2560,1280]{2,1,0:T(8,128)(2,1)} %slice.18) | data formatting | bytes 52428800
  929.6 2.9 slice-done.4
  932.5 93.4 %copy.59 = bf16[1,2560,1280]{2,0,1:T(2,128)(2,1)S(1)} copy(bf16[1,2560,1280]{2,1,0:T(8,128)(2,1)S(1)} %slice-done.4) | data formatting | bytes 13107200
  1025.9 78.5 %fusion.11 = f32[2,7]{1,0:T(2,128)S(1)} fusion(bf16[2,2560,1280]{2,0,1:T(2,128)(2,1)} %copy.50, bf16[1,2560,1280]{2,0,1:T(2,128)(2,1)S(1)} %copy.59, bf16[1,2560,1280]{2,0,1:T(2,128)(2,1)} %copy.49, bf16[1,2560,1280]{2,0,1:T(2,128)(2,1)} %copy.48, bf16[4,2560,1280]{2,0,1:T(4,128)(2,1)} %copy.58), kind=kOutput, calls=%fused_computation.34 | convolution fusion | flops 275251200 | bytes 58982456 | tf_op jit(solution)/shard_map/ead,kad->ek/dot_general | solution.py:78
  1104.5 11.7 %psum.63 = f32[2,7]{1,0:T(2,128)S(1)} all-reduce(f32[2,7]{1,0:T(2,128)S(1)} %fusion.11), channel_id=1, replica_groups=mesh['dp'=8,'tensor'=4] {'tensor'}, use_global_device_ids=true, to_apply=%region_20.0 | all-reduce | flops 14 | bytes 112 | tf_op jit(solution)/shard_map/psum | solution.py:81
  (51 shorter events, 5.7 us)
Async XLA Ops:
  7.2 53.0 %all-gather.5.cloned.1.call-start = ((), (), s32[]{:S(2)}) async-start(), calls=%async_computation.2 | async-start | bytes 7372800 | tf_op jit(solution)/shard_map/all_gather | solution.py:30
  7.9 101.3 %all-gather.7.cloned.1.call-start = ((), (), s32[]{:S(2)}) async-start(), calls=%async_computation.3 | async-start | bytes 7372800 | tf_op jit(solution)/shard_map/all_gather | solution.py:43
  56.2 277.3 %copy-start = (f32[1,320,1280]{2,1,0:T(8,128)}, f32[1,320,1280]{2,1,0:T(8,128)S(1)}, u32[]{:S(2)}) copy-start(f32[1,320,1280]{2,1,0:T(8,128)S(1)} %get-tuple-element.20) | copy-start | bytes 4915204
  56.2 186.3 %reduce-scatter.7.cloned.1.call-start = ((), (), s32[]{:S(2)}) async-start(), calls=%async_computation.6 | async-start | bytes 14745600 | tf_op jit(solution)/shard_map/reduce_scatter | solution.py:47
  147.2 280.3 %all-gather.9.cloned.1.call-start = ((), (), s32[]{:S(2)}) async-start(), calls=%async_computation.4 | async-start | bytes 7372800 | tf_op jit(solution)/shard_map/all_gather | solution.py:43
  286.1 3.9 copy-start.7
  286.1 4.6 slice-start
  286.1 5.3 slice-start.1
  380.0 180.9 %reduce-scatter.9.cloned.1.call-start = ((), (), s32[]{:S(2)}) async-start(), calls=%async_computation.7 | async-start | bytes 14745600 | tf_op jit(solution)/shard_map/reduce_scatter | solution.py:47
  465.6 412.3 %all-gather.11.cloned.1.call-start = ((), (), s32[]{:S(2)}) async-start(), calls=%async_computation.5 | async-start | bytes 36864000 | tf_op jit(solution)/shard_map/all_gather | solution.py:76
  560.9 61.3 %slice-start.2 = ((s8[6553600]{0:T(1024)(128)(4,1)}), s8[2359296]{0:T(1024)(128)(4,1)S(1)}, s32[]{:S(2)}) async-start(s8[6553600]{0:T(1024)(128)(4,1)} %bitcast.48), calls=%async_computation.10 | async-start | bytes 4718592
  616.2 4.6 copy-start.9
  616.2 5.9 slice-start.3
  620.8 2.3 copy-start.1
  620.9 2.8 copy-start.2
  621.0 1.1 copy-start.4
  667.6 4.5 copy-start.5
  672.2 45.1 %copy-start.6 = (bf16[4,320,1280]{2,1,0:T(8,128)(2,1)S(1)}, bf16[4,320,1280]{2,1,0:T(8,128)(2,1)}, u32[]{:S(2)}) copy-start(bf16[4,320,1280]{2,1,0:T(8,128)(2,1)} %slice.14) | copy-start | bytes 9830404
  779.1 13.4 %copy-start.3 = (f32[1,320,1280]{2,1,0:T(8,128)S(1)}, f32[1,320,1280]{2,1,0:T(8,128)}, u32[]{:S(2)}) copy-start(f32[1,320,1280]{2,1,0:T(8,128)} %get-tuple-element.18) | copy-start | bytes 4915204
  779.1 13.4 %copy-start.8 = (f32[1,320,1280]{2,1,0:T(8,128)S(1)}, f32[1,320,1280]{2,1,0:T(8,128)}, u32[]{:S(2)}) copy-start(f32[1,320,1280]{2,1,0:T(8,128)} %get-tuple-element.13) | copy-start | bytes 4915204
  929.6 2.9 slice-start.4
Sparse Core Ops, SparseCore 0:
  9.9 50.1 all-gather.4
  62.6 46.5 all-gather.6
  147.4 95.1 reduce-scatter.6
  380.1 47.3 all-gather.8
  465.7 95.1 reduce-scatter.8
  719.7 158.2 all-gather.10
where the time goes:
time: 1130 us; the launch traced here: 1120 us
  waiting for transfers between devices  362 us (32%)
  blocking collectives  304 us (27%)
  local copies, waits for them, and re-layouts  238 us (21%)
  matrix products  153 us (14%)
  other arithmetic  49.3 us (4%)
  between operations  16.5 us (1%)
    reduce_scatter x2, waiting for transfers between devices, shards(): lax.psum_scatter(lax.dot_general(activations, scaled, (((0,), (0,)), ((),...  191 us
    unnamed x32, local copies, waits for them, and re-layouts  159 us
    psum x2, blocking collectives, shards(): lax.psum(local_products(vectors, imaged), ('dp', 'tensor')) / nparam  89.7 us
    all_gather x1, waiting for transfers between devices, shards(): full_extra = lax.all_gather(extra_rows, 'dp', axis=1, tiled=True)  83.5 us
    all_gather x2, waiting for transfers between devices, shards(): gathered_dir = lax.all_gather(direction, 'dp', axis=0, tiled=True)  83.4 us
    psum x2, blocking collectives, shards(): lax.psum(local_products(vectors, remainder), ('dp', 'tensor')) / nparam  81.4 us
    psum x2, blocking collectives, shards(): lax.psum(jnp.sum(remainder * remainder), ('dp', 'tensor')) / nparam  78.9 us
    dot_general x1, matrix products, shards(): jnp.einsum('ead,kad->ek', grads, basis_table, preferred_element_type=jnp....  78.5 us
  transfers between devices with their start and end apart: 6, of which 6 were waited for; matrix products, arithmetic and copies ran while one was open for 8% of the time, Pallas kernels for 0%

commit v1 on v0

v1 whole, which is shorter than its diff:
```python
import math

import jax
import jax.numpy as jnp
from jax import lax
from jax.sharding import PartitionSpec as P

ITERS = 2
BOTH = ("dp", "tensor")


def dots(vectors, one):
    return [jnp.sum(v * one) for v in vectors]


def orthogonalize(vectors, imaged, firsts, square, gram):
    second = firsts - jnp.sum(gram * firsts[None, :], axis=1)
    total = firsts + second
    rest = square - 2.0 * jnp.sum(total * firsts) + jnp.sum(
        total[:, None] * gram * total[None, :]
    )
    norm = jnp.sqrt(rest)
    remainder = imaged
    for k, v in enumerate(vectors):
        remainder = remainder - total[k] * v
    return remainder / norm, jnp.concatenate([total, norm[None]])


def shards(activations, weight, target, start_vector, stored):
    rows = activations.shape[0]
    ndp = lax.axis_size("dp")
    total_rows = rows * ndp
    nparam = float(weight.shape[0] * ndp * weight.shape[1] * lax.axis_size("tensor"))
    tok_ex = 512
    examples = rows // tok_ex
    ks = stored.shape[0]

    square_sum = lax.psum(jnp.sum(start_vector * start_vector), BOTH) / nparam
    q0 = start_vector / jnp.sqrt(square_sum)
    full_weight, q0 = lax.optimization_barrier(
        (lax.all_gather(weight, "dp", axis=0, tiled=True), q0)
    )
    hidden = jnp.dot(activations, full_weight, preferred_element_type=jnp.float32)
    slope = jnp.tanh(hidden - target.astype(jnp.float32))
    curvature = (1.0 - slope * slope) / total_rows
    signs = slope.astype(jnp.bfloat16)

    def project(mapped):
        part = signs.astype(jnp.float32) * mapped
        return jnp.sum(part.reshape(examples, -1), axis=1)

    def gather(v):
        return lax.all_gather(v, "dp", axis=v.ndim - 2, tiled=True)

    def image(v):
        return jnp.dot(activations, v, preferred_element_type=jnp.float32)

    def hessian(v):
        mapped = image(gather(v.astype(jnp.bfloat16)))
        scaled = (curvature * mapped).astype(jnp.bfloat16)
        part = jnp.dot(activations.T, scaled, preferred_element_type=jnp.float32)
        imaged = lax.psum_scatter(part, "dp", scatter_dimension=0, tiled=True)
        return imaged, project(mapped)

    vectors = [stored[k] for k in range(ks)] + [q0]
    table = stored.astype(jnp.bfloat16)
    half = ks // 2

    w, proj_q0 = hessian(q0)
    gram_local = []
    for i in range(ks + 1):
        for j in range(i + 1):
            gram_local.append(jnp.sum(vectors[i] * vectors[j]))
    table_a, _ = lax.optimization_barrier((table[:half], w[0, 0]))
    full_a = gather(table_a)
    sums = lax.psum(
        jnp.stack(dots(vectors, w) + [jnp.sum(w * w)] + gram_local), BOTH
    ) / nparam
    n = ks + 1
    index = [[0] * n for _ in range(n)]
    count = 0
    for i in range(n):
        for j in range(i + 1):
            index[i][j] = index[j][i] = n + 1 + count
            count += 1
    gram = jnp.stack([jnp.stack([sums[index[i][j]] for j in range(n)]) for i in range(n)])
    q1, coef_first = orthogonalize(vectors, w, sums[:n], sums[n], gram)

    w, proj_q1 = hessian(q1)
    cross_local = dots(vectors, q1) + [jnp.sum(q1 * q1)]
    vectors = vectors + [q1]
    table_b, _ = lax.optimization_barrier((table[half:], w[0, 0]))
    full_b = gather(table_b)
    m = n + 1
    sums = lax.psum(
        jnp.stack(dots(vectors, w) + [jnp.sum(w * w)] + cross_local), BOTH
    ) / nparam
    cross = sums[m + 1 :]
    gram = jnp.concatenate(
        [jnp.concatenate([gram, cross[:n, None]], axis=1), cross[None, :]], axis=0
    )
    q2, coef_second = orthogonalize(vectors, w, sums[:m], sums[m], gram)

    parts = [project(image(full_a[k])) for k in range(half)]
    parts += [project(image(full_b[k])) for k in range(ks - half)]
    parts += [proj_q0, proj_q1, project(image(gather(q2.astype(jnp.bfloat16))))]
    projections = lax.psum(jnp.stack(parts, axis=1), "tensor")
    projections = projections / math.sqrt(float(tok_ex) * nparam)
    return (jnp.stack([q1, q2]), coef_first, coef_second, projections)


def solution(mesh):
    in_specs = (
        P("dp", None),
        P("dp", "tensor"),
        P("dp", "tensor"),
        P("dp", "tensor"),
        P(None, "dp", "tensor"),
    )
    out_specs = (P(None, "dp", "tensor"), P(), P(), P("dp", None))
    return jax.shard_map(shards, mesh=mesh, in_specs=in_specs, out_specs=out_specs, check_vma=False)
```

time: 1130 us -> 756 us (0.67)
  blocking collectives: 304 us -> 133 us
  local copies, waits for them, and re-layouts: 238 us -> 68.2 us
  matrix products: 153 us -> 123 us
  waiting for transfers between devices: 362 us -> 349 us
    psum x8 -> x4, blocking collectives: 304 us -> 133 us  [the longest x1 42.6 us: shards(): square_sum = lax.psum(jnp.sum(start_vector * start_vector), BOTH) / nparam]
    unnamed x32 -> x17, local copies, waits for them, and re-layouts: 159 us -> 40.2 us
    convert_element_type x1 -> x0, local copies, waits for them, and re-layouts: 32.7 us -> none  [shards(): grads = jnp.einsum('eta,etd->ead', example_rows, example_signs, preferred...]
    dot_general x7 -> x10, matrix products: 153 us -> 123 us  [the longest x7 83.9 us: image(): return jnp.dot(activations, v, preferred_element_type=jnp.float32)]
    convert_element_type x0 -> x4, other arithmetic: none -> 21.8 us  [the longest x1 9.47 us: shards(): parts += [proj_q0, proj_q1, project(image(gather(q2.astype(jnp.bfloat16))))]]
    slice x3 -> x9, local copies, waits for them, and re-layouts: 21 us -> 4.8 us  [the longest x1 1.91 us: shards(): table_b, _ = lax.optimization_barrier((table[half:], w[0, 0]))]
    reduce_sum x11 -> x16, other arithmetic: 34.1 us -> 19.8 us  [the longest x2 5.56 us: shards(): jnp.sum(w * w)]
    all_gather x3 -> x5, waiting for transfers between devices: 167 us -> 157 us  [gather(): return lax.all_gather(v, 'dp', axis=v.ndim - 2, tiled=True)]
  transfers between devices with their start and end apart: 6 -> 8, of which waited for: 6 -> 8; matrix products, arithmetic and copies ran while one was open for 8% -> 14% of each run, Pallas kernels for 0% -> 0%
where the time goes in v1:
time: 756 us; the launch traced here: 746 us
  waiting for transfers between devices  349 us (46%)
  blocking collectives  133 us (18%)
  matrix products  123 us (16%)
  local copies, waits for them, and re-layouts  68.2 us (9%)
  other arithmetic  52.6 us (7%)
  between operations  19.4 us (3%)
    reduce_scatter x2, waiting for transfers between devices, hessian(): imaged = lax.psum_scatter(part, 'dp', scatter_dimension=0, tiled=True)  184 us
    all_gather x5, waiting for transfers between devices, gather(): return lax.all_gather(v, 'dp', axis=v.ndim - 2, tiled=True)  157 us
    dot_general x7, matrix products, image(): return jnp.dot(activations, v, preferred_element_type=jnp.float32)  83.9 us
    psum x1, blocking collectives, shards(): square_sum = lax.psum(jnp.sum(start_vector * start_vector), BOTH) / nparam  42.6 us
    unnamed x17, local copies, waits for them, and re-layouts  40.2 us
    psum x1, blocking collectives, shards(): lax.psum(jnp.stack(dots(vectors, w) + [jnp.sum(w * w)] + cross_local), BOTH)  39.6 us
    psum x1, blocking collectives, shards(): lax.psum(jnp.stack(dots(vectors, w) + [jnp.sum(w * w)] + gram_local), BOTH)  39.3 us
    dot_general x2, matrix products, hessian(): part = jnp.dot(activations.T, scaled, preferred_element_type=jnp.float32)  25.5 us
  transfers between devices with their start and end apart: 8, of which 8 were waited for; matrix products, arithmetic and copies ran while one was open for 14% of the time, Pallas kernels for 0%

profile of v1, /device:TPU:0, one launch (start us, length us, event | category | flops | bytes accessed | tf_op | source)
XLA Modules:
  0.0 745.6 jit_solution(1846878476665788876)
XLA Ops:
  7.2 0.7 all-gather.7.cloned.1.call-update
  8.0 2.5 multiply_reduce_fusion.8
  10.4 42.6 %psum.28 = f32[]{:T(128)} all-reduce(f32[]{:T(128)} %multiply_reduce_fusion.8), channel_id=1, replica_groups=mesh['dp'=8,'tensor'=4] {'dp','tensor'}, use_global_device_ids=true, to_apply=%region_1.0 | all-reduce | flops 1 | bytes 8 | tf_op jit(solution)/shard_map/psum | solution.py:38
  53.8 6.3 all-gather.7.cloned.1.call-done
  60.1 1.0 convert_element_type.34
  61.2 4.4 copy.48
  65.6 13.5 %fusion.13 = f32[1024,1280]{0,1:T(8,128)} fusion(bf16[1024,1280]{0,1:T(8,128)(2,1)} %copy.48, bf16[2560,1280]{1,0:T(8,128)(2,1)} %all-gather.7.cloned.1.call-done, bf16[1024,2560]{1,0:T(8,128)(2,1)} %param.5), kind=kOutput, calls=%fused_computation.29 | convolution fusion | flops 6713507840 | bytes 19660800 | tf_op jit(solution)/shard_map/dot_general | solution.py:43
  79.1 29.5 %all-gather.9.cloned.1.call-done = bf16[2560,1280]{1,0:T(8,128)(2,1)} async-done(((bf16[320,1280]{1,0:T(8,128)(2,1)}), bf16[2560,1280]{1,0:T(8,128)(2,1)}) %all-gather.9.cloned.1.call-update) | async-done | bytes 6553616 | tf_op jit(solution)/shard_map/all_gather | solution.py:53
  108.6 10.8 %fusion.73 = f32[1280,1024]{1,0:T(8,128)S(1)} fusion(bf16[2560,1280]{1,0:T(8,128)(2,1)} %all-gather.9.cloned.1.call-done, bf16[1024,2560]{1,0:T(8,128)(2,1)} %param.5), kind=kOutput, calls=%fused_computation.152 | convolution fusion | flops 6710886400 | bytes 17039360 | tf_op jit(solution)/shard_map/dot_general | solution.py:56
  119.5 2.3 copy-done.5
  121.7 12.4 %convolution_bitcast_fusion.1 = f32[2560,1280]{0,1:T(8,128)} fusion(bf16[1024,2560]{1,0:T(8,128)(2,1)} %param.5, f32[1280,1024]{1,0:T(8,128)S(1)} %fusion.73, f32[1024,1280]{0,1:T(8,128)S(1)} %copy-done.4), kind=kOutput, calls=%fused_computation.8 | convolution fusion | flops 6717440000 | bytes 28835840 | tf_op jit(solution)/shard_map/dot_general | solution.py:61
  134.1 14.0 %copy.78 = f32[2560,1280]{1,0:T(8,128)} copy(f32[2560,1280]{0,1:T(8,128)} %convolution_bitcast_fusion.1) | data formatting | bytes 26214400
  148.3 95.1 %reduce-scatter.7.cloned.1.call-done = f32[320,1280]{1,0:T(8,128)} async-done(((f32[2560,1280]{1,0:T(8,128)}), f32[320,1280]{1,0:T(8,128)}) %reduce-scatter.7.cloned.1.call-update) | async-done | bytes 1638416 | tf_op jit(solution)/shard_map/reduce_scatter | solution.py:62
  243.4 2.9 copy.79
  246.3 2.7 multiply_reduce_fusion.1
  249.0 4.8 fusion.25
  253.8 13.6 %stack.198 = f32[21]{0:T(128)S(1)} concatenate(f32[1]{0:T(128)} %bitcast.4, f32[1]{0:T(128)} %bitcast.6, f32[1]{0:T(128)} %bitcast.8, f32[1]{0:T(128)} %bitcast.10, f32[1]{0:T(128)} %bitcast.11, f32[1]{0:T(128)} %bitcast.12, f32[1]{0:T(128)} %bitcast.13, f32[1]{0:T(128)} %bitcast.14, f32[1]{0:T(128)} %bitcast.15, f32[1]{0:T(128)} %bitcast.16, f32[1]{0:T(128)} %bitcast.17, ...), dimensions={0} | concatenate | bytes 168 | tf_op jit(solution)/shard_map/stack | solution.py:77
  267.4 39.3 %psum.29 = f32[21]{0:T(128)S(1)} all-reduce(f32[21]{0:T(128)S(1)} %stack.198), channel_id=1, replica_groups=mesh['dp'=8,'tensor'=4] {'dp','tensor'}, use_global_device_ids=true, to_apply=%region_24.0 | all-reduce | flops 21 | bytes 168 | tf_op jit(solution)/shard_map/psum | solution.py:76
  306.8 0.7 fusion.71
  307.8 2.0 maximum_bitcast_fusion.2
  309.8 4.0 maximum_bitcast_fusion
  315.2 0.7 multiply_reduce_fusion.11
  317.8 8.1 %fusion.65 = (bf16[320,1280]{1,0:T(8,128)(2,1)}, f32[320,1280]{1,0:T(8,128)S(1)}) fusion(f32[]{:T(128)} %sqrt.10, f32[320,1280]{1,0:T(8,128)S(1)} %broadcast_divide_fusion, f32[]{:T(128)} %bitcast.37, f32[4,320,1280]{2,1,0:T(8,128)} %param.9, f32[]{:T(128)} %bitcast.36, f32[]{:T(128)} %bitcast.35, f32[]{:T(128)} %bitcast.34, ...), kind=kLoop, calls=%fused_computation.145 | loop fusion | flops 4915200 | bytes 12288024 | tf_op jit(solution)/shard_map/convert_element_type | solution.py:59
  326.0 47.3 %all-gather.11.cloned.1.call-done = bf16[2560,1280]{1,0:T(8,128)(2,1)} async-done(((bf16[320,1280]{1,0:T(8,128)(2,1)}), bf16[2560,1280]{1,0:T(8,128)(2,1)}) %all-gather.11.cloned.1.call-update) | async-done | bytes 6553616 | tf_op jit(solution)/shard_map/all_gather | solution.py:53
  373.4 16.5 %fusion.9 = (f32[1024]{0:T(1024)S(1)}, f32[1024]{0:T(1024)S(1)}, bf16[1024,1280]{0,1:T(8,128)(2,1)}, f32[1280,1024]{1,0:T(8,128)S(1)}) fusion(f32[1280,1024]{1,0:T(8,128)} %copy-done.5, f32[1024,1280]{0,1:T(8,128)} %fusion.13, bf16[2560,1280]{1,0:T(8,128)(2,1)} %all-gather.11.cloned.1.call-done, bf16[1024,2560]{1,0:T(8,128)(2,1)} %param.5), kind=kOutput, calls=%fused_computation.22 | convolution fusion | flops 6718748672 | bytes 30154752 | tf_op jit(solution)/shard_map/dot_general | solution.py:56
  389.8 13.1 %convolution_bitcast_fusion = f32[2560,1280]{0,1:T(8,128)} fusion(bf16[1024,2560]{1,0:T(8,128)(2,1)} %param.5, f32[1280,1024]{1,0:T(8,128)S(1)} %get-tuple-element.95, f32[1024,1280]{0,1:T(8,128)} %fusion.13), kind=kOutput, calls=%fused_computation.7 | convolution fusion | flops 6717440000 | bytes 28835840 | tf_op jit(solution)/shard_map/dot_general | solution.py:61
  402.9 13.9 %copy.80 = f32[2560,1280]{1,0:T(8,128)} copy(f32[2560,1280]{0,1:T(8,128)} %convolution_bitcast_fusion) | data formatting | bytes 26214400
  416.9 3.2 convert_element_type.40
  420.1 1.9 fusion.67
  422.1 0.7 all-gather.15.cloned.1.call-update
  423.0 89.1 %reduce-scatter.9.cloned.1.call-done = f32[320,1280]{1,0:T(8,128)} async-done(((f32[2560,1280]{1,0:T(8,128)}), f32[320,1280]{1,0:T(8,128)}) %reduce-scatter.9.cloned.1.call-update) | async-done | bytes 1638416 | tf_op jit(solution)/shard_map/reduce_scatter | solution.py:62
  512.2 2.8 copy.81
  515.0 2.9 multiply_reduce_fusion
  517.8 4.5 fusion.30
  522.3 8.5 %stack.223 = f32[13]{0:T(128)S(1)} concatenate(f32[1]{0:T(128)} %bitcast.42, f32[1]{0:T(128)} %bitcast.43, f32[1]{0:T(128)} %bitcast.44, f32[1]{0:T(128)} %bitcast.45, f32[1]{0:T(128)} %bitcast.46, f32[1]{0:T(128)} %bitcast.47, f32[1]{0:T(128)} %bitcast.48, f32[1]{0:T(128)} %bitcast.49, f32[1]{0:T(128)} %bitcast.50, f32[1]{0:T(128)} %bitcast.51, f32[1]{0:T(128)} %bitcast.52, ...), dimensions={0} | concatenate | bytes 104 | tf_op jit(solution)/shard_map/stack | solution.py:96
  530.8 39.6 %psum.30 = f32[13]{0:T(128)S(1)} all-reduce(f32[13]{0:T(128)S(1)} %stack.223), channel_id=1, replica_groups=mesh['dp'=8,'tensor'=4] {'dp','tensor'}, use_global_device_ids=true, to_apply=%region_42.0 | all-reduce | flops 13 | bytes 104 | tf_op jit(solution)/shard_map/psum | solution.py:95
  573.3 0.7 multiply_reduce_fusion.9
  575.3 9.5 %fusion.63 = (bf16[320,1280]{1,0:T(8,128)(2,1)}, f32[320,1280]{1,0:T(8,128)}) fusion(f32[]{:T(128)} %sqrt.11, f32[320,1280]{1,0:T(8,128)S(1)} %get-tuple-element.54, f32[]{:T(128)} %bitcast.62, f32[320,1280]{1,0:T(8,128)S(1)} %broadcast_divide_fusion, f32[]{:T(128)} %bitcast.61, f32[4,320,1280]{2,1,0:T(8,128)} %param.9, f32[]{:T(128)} %bitcast.60, ...), kind=kLoop, calls=%fused_computation.144 | loop fusion | flops 5734400 | bytes 13926428 | tf_op jit(solution)/shard_map/convert_element_type | solution.py:106
  585.4 4.2 all-gather.13.cloned.1.call-done
  589.6 11.1 %fusion.4 = f32[1024]{0:T(1024)S(1)} fusion(bf16[1024,1280]{0,1:T(8,128)(2,1)} %get-tuple-element.52, bf16[1024,2560]{1,0:T(8,128)(2,1)} %param.5, bf16[2,2560,1280]{2,1,0:T(8,128)(2,1)} %all-gather.13.cloned.1.call-done), kind=kOutput, calls=%fused_computation.17 | convolution fusion | flops 6714817536 | bytes 14422016 | tf_op jit(solution)/shard_map/dot_general | solution.py:56
  601.0 11.6 %fusion.5 = f32[1024]{0:T(1024)S(1)} fusion(bf16[1024,1280]{0,1:T(8,128)(2,1)} %get-tuple-element.52, bf16[1024,2560]{1,0:T(8,128)(2,1)} %param.5, bf16[2,2560,1280]{2,1,0:T(8,128)(2,1)} %all-gather.13.cloned.1.call-done), kind=kOutput, calls=%fused_computation.18 | convolution fusion | flops 6714817536 | bytes 14422016 | tf_op jit(solution)/shard_map/dot_general | solution.py:56
  612.8 53.1 %all-gather.15.cloned.1.call-done = bf16[2,2560,1280]{2,1,0:T(8,128)(2,1)} async-done(((bf16[2,320,1280]{2,1,0:T(8,128)(2,1)}), bf16[2,2560,1280]{2,1,0:T(8,128)(2,1)}) %all-gather.15.cloned.1.call-update) | async-done | bytes 13107216 | tf_op jit(solution)/shard_map/all_gather | solution.py:53
  665.9 11.4 %fusion.6 = f32[1024]{0:T(1024)S(1)} fusion(bf16[1024,1280]{0,1:T(8,128)(2,1)} %get-tuple-element.52, bf16[1024,2560]{1,0:T(8,128)(2,1)} %param.5, bf16[2,2560,1280]{2,1,0:T(8,128)(2,1)} %all-gather.15.cloned.1.call-done), kind=kOutput, calls=%fused_computation.19 | convolution fusion | flops 6714817536 | bytes 14422016 | tf_op jit(solution)/shard_map/dot_general | solution.py:56
  677.5 11.2 %fusion.7 = f32[1024]{0:T(1024)S(1)} fusion(bf16[1024,1280]{0,1:T(8,128)(2,1)} %get-tuple-element.52, bf16[1024,2560]{1,0:T(8,128)(2,1)} %param.5, bf16[2,2560,1280]{2,1,0:T(8,128)(2,1)} %all-gather.15.cloned.1.call-done), kind=kOutput, calls=%fused_computation.20 | convolution fusion | flops 6714817536 | bytes 14422016 | tf_op jit(solution)/shard_map/dot_general | solution.py:56
  690.0 1.9 pad_maximum_fusion
  692.0 22.5 %all-gather.17.cloned.1.call-done = bf16[2560,1280]{1,0:T(8,128)(2,1)} async-done(((bf16[320,1280]{1,0:T(8,128)(2,1)}), bf16[2560,1280]{1,0:T(8,128)(2,1)}) %all-gather.17.cloned.1.call-update) | async-done | bytes 6553616 | tf_op jit(solution)/shard_map/all_gather | solution.py:53
  714.4 11.3 %fusion.10 = f32[1024]{0:T(1024)S(1)} fusion(bf16[1024,1280]{0,1:T(8,128)(2,1)} %get-tuple-element.52, bf16[2560,1280]{1,0:T(8,128)(2,1)} %all-gather.17.cloned.1.call-done, bf16[1024,2560]{1,0:T(8,128)(2,1)} %param.5), kind=kOutput, calls=%fused_computation.23 | convolution fusion | flops 6714817536 | bytes 14422016 | tf_op jit(solution)/shard_map/dot_general | solution.py:56
  726.1 11.7 %psum.31 = f32[2,7]{1,0:T(2,128)S(1)} all-reduce(f32[2,7]{1,0:T(2,128)S(1)} %stack.233), channel_id=1, replica_groups=mesh['dp'=8,'tensor'=4] {'tensor'}, use_global_device_ids=true, to_apply=%region_60.61 | all-reduce | flops 14 | bytes 112 | tf_op jit(solution)/shard_map/psum | solution.py:107
  (68 shorter events, 8.4 us)
Async XLA Ops:
  7.2 46.5 %copy-start.3 = (f32[320,1280]{1,0:T(8,128)S(1)}, f32[320,1280]{1,0:T(8,128)}, u32[]{:S(2)}) copy-start(f32[320,1280]{1,0:T(8,128)} %param.8) | copy-start | bytes 4915204
  7.2 53.0 %all-gather.7.cloned.1.call-start = ((), (), s32[]{:S(2)}) async-start(), calls=%async_computation.2 | async-start | bytes 7372800 | tf_op jit(solution)/shard_map/all_gather | solution.py:41
  7.9 100.7 %all-gather.9.cloned.1.call-start = ((), (), s32[]{:S(2)}) async-start(), calls=%async_computation.3 | async-start | bytes 7372800 | tf_op jit(solution)/shard_map/all_gather | solution.py:53
  61.2 182.2 %reduce-scatter.7.cloned.1.call-start = ((), (), s32[]{:S(2)}) async-start(), calls=%async_computation.8 | async-start | bytes 14745600 | tf_op jit(solution)/shard_map/reduce_scatter | solution.py:62
  108.6 13.1 %copy-start.4 = (f32[1024,1280]{0,1:T(8,128)S(1)}, f32[1024,1280]{0,1:T(8,128)}, u32[]{:S(2)}) copy-start(f32[1024,1280]{0,1:T(8,128)} %fusion.13) | copy-start | bytes 15728644
  119.4 2.3 copy-start.5
  148.1 225.3 %all-gather.11.cloned.1.call-start = ((), (), s32[]{:S(2)}) async-start(), calls=%async_computation.4 | async-start | bytes 7372800 | tf_op jit(solution)/shard_map/all_gather | solution.py:53
  243.4 5.6 copy-start
  326.0 186.2 %reduce-scatter.9.cloned.1.call-start = ((), (), s32[]{:S(2)}) async-start(), calls=%async_computation.9 | async-start | bytes 14745600 | tf_op jit(solution)/shard_map/reduce_scatter | solution.py:62
  416.9 172.8 %all-gather.13.cloned.1.call-start = ((), (), s32[]{:S(2)}) async-start(), calls=%async_computation.5 | async-start | bytes 14745600 | tf_op jit(solution)/shard_map/all_gather | solution.py:53
  422.0 243.9 %all-gather.15.cloned.1.call-start = ((), (), s32[]{:S(2)}) async-start(), calls=%async_computation.6 | async-start | bytes 14745600 | tf_op jit(solution)/shard_map/all_gather | solution.py:53
  422.8 291.7 %all-gather.17.cloned.1.call-start = ((), (), s32[]{:S(2)}) async-start(), calls=%async_computation.7 | async-start | bytes 7372800 | tf_op jit(solution)/shard_map/all_gather | solution.py:53
  515.0 2.9 copy-start.1
  677.5 12.5 %copy-start.2 = (f32[320,1280]{1,0:T(8,128)S(1)}, f32[320,1280]{1,0:T(8,128)}, u32[]{:S(2)}) copy-start(f32[320,1280]{1,0:T(8,128)} %get-tuple-element.51) | copy-start | bytes 4915204
Sparse Core Ops, SparseCore 0:
  9.9 50.1 all-gather.6
  62.0 46.5 all-gather.8
  148.2 95.1 reduce-scatter.6
  326.1 47.2 all-gather.10
  417.0 95.1 reduce-scatter.8
  513.9 75.6 all-gather.12
  591.5 74.3 all-gather.14
  667.8 46.6 all-gather.16

commit v2 on v1

--- a/solution.py
+++ b/solution.py
@@ -10,7 +10,7 @@
 
 
 def dots(vectors, one):
-    return [jnp.sum(v * one) for v in vectors]
+    return jnp.sum(jnp.stack(vectors) * one[None], axis=(1, 2))
 
 
 def orthogonalize(vectors, imaged, firsts, square, gram):
@@ -59,47 +59,38 @@
         mapped = image(gather(v.astype(jnp.bfloat16)))
         scaled = (curvature * mapped).astype(jnp.bfloat16)
         part = jnp.dot(activations.T, scaled, preferred_element_type=jnp.float32)
-        imaged = lax.psum_scatter(part, "dp", scatter_dimension=0, tiled=True)
-        return imaged, project(mapped)
+        imaged = lax.psum_scatter(
+            part.astype(jnp.bfloat16), "dp", scatter_dimension=0, tiled=True
+        )
+        return imaged.astype(jnp.float32), project(mapped)
 
     vectors = [stored[k] for k in range(ks)] + [q0]
     table = stored.astype(jnp.bfloat16)
     half = ks // 2
 
     w, proj_q0 = hessian(q0)
-    gram_local = []
-    for i in range(ks + 1):
-        for j in range(i + 1):
-            gram_local.append(jnp.sum(vectors[i] * vectors[j]))
+    n = ks + 1
     table_a, _ = lax.optimization_barrier((table[:half], w[0, 0]))
     full_a = gather(table_a)
-    sums = lax.psum(
-        jnp.stack(dots(vectors, w) + [jnp.sum(w * w)] + gram_local), BOTH
-    ) / nparam
-    n = ks + 1
-    index = [[0] * n for _ in range(n)]
-    count = 0
-    for i in range(n):
-        for j in range(i + 1):
-            index[i][j] = index[j][i] = n + 1 + count
-            count += 1
-    gram = jnp.stack([jnp.stack([sums[index[i][j]] for j in range(n)]) for i in range(n)])
+    gram_rows = [dots(vectors, v) for v in vectors]
+    sums = lax.psum(jnp.concatenate([dots(vectors + [w], w)] + gram_rows), BOTH) / nparam
+    gram = sums[n + 1 :].reshape(n, n)
     q1, coef_first = orthogonalize(vectors, w, sums[:n], sums[n], gram)
 
+    full_a, q1 = lax.optimization_barrier((full_a, q1))
+    vectors = vectors + [q1]
     w, proj_q1 = hessian(q1)
-    cross_local = dots(vectors, q1) + [jnp.sum(q1 * q1)]
-    vectors = vectors + [q1]
+    cross = dots(vectors, q1)
+    m = n + 1
     table_b, _ = lax.optimization_barrier((table[half:], w[0, 0]))
     full_b = gather(table_b)
-    m = n + 1
-    sums = lax.psum(
-        jnp.stack(dots(vectors, w) + [jnp.sum(w * w)] + cross_local), BOTH
-    ) / nparam
+    sums = lax.psum(jnp.concatenate([dots(vectors + [w], w), cross]), BOTH) / nparam
     cross = sums[m + 1 :]
     gram = jnp.concatenate(
         [jnp.concatenate([gram, cross[:n, None]], axis=1), cross[None, :]], axis=0
     )
     q2, coef_second = orthogonalize(vectors, w, sums[:m], sums[m], gram)
+    full_b, q2 = lax.optimization_barrier((full_b, q2))
 
     parts = [project(image(full_a[k])) for k in range(half)]
     parts += [project(image(full_b[k])) for k in range(ks - half)]

time: 756 us -> 606 us (0.80)
  waiting for transfers between devices: 349 us -> 227 us
  local copies, waits for them, and re-layouts: 68.2 us -> 35.2 us
    reduce_scatter x2, waiting for transfers between devices: 184 us -> 105 us  [hessian(): lax.psum_scatter(part.astype(jnp.bfloat16), 'dp', scatter_dimension=0, ti...]
    all_gather x5, waiting for transfers between devices: 157 us -> 116 us  [gather(): return lax.all_gather(v, 'dp', axis=v.ndim - 2, tiled=True)]
    another operation x3 -> x0, local copies, waits for them, and re-layouts: 22.1 us -> none  [the longest x1 13.6 us: shards(): jnp.stack(dots(vectors, w) + [jnp.sum(w * w)] + gram_local)]
    div x2 -> x4, other arithmetic: 0.01 us -> 15.9 us  [the longest x2 15.9 us: orthogonalize(): return (remainder / norm, jnp.concatenate([total, norm[None]]))]
    unnamed x17 -> x9, local copies, waits for them, and re-layouts: 40.2 us -> 25.7 us
  transfers between devices with their start and end apart: 8 -> 8, of which waited for: 8 -> 7; matrix products, arithmetic and copies ran while one was open for 14% -> 21% of each run, Pallas kernels for 0% -> 0%
where the time goes in v2:
time: 606 us; the launch traced here: 596 us
  waiting for transfers between devices  227 us (37%)
  blocking collectives  134 us (22%)
  matrix products  122 us (20%)
  other arithmetic  57.1 us (9%)
  local copies, waits for them, and re-layouts  35.2 us (6%)
  between operations  19.1 us (3%)
    all_gather x5, waiting for transfers between devices, gather(): return lax.all_gather(v, 'dp', axis=v.ndim - 2, tiled=True)  116 us
    reduce_scatter x2, waiting for transfers between devices, hessian(): lax.psum_scatter(part.astype(jnp.bfloat16), 'dp', scatter_dimension=0, ti...  105 us
    dot_general x7, matrix products, image(): return jnp.dot(activations, v, preferred_element_type=jnp.float32)  85.3 us
    psum x1, blocking collectives, shards(): square_sum = lax.psum(jnp.sum(start_vector * start_vector), BOTH) / nparam  42.6 us
    psum x1, blocking collectives, shards(): lax.psum(jnp.concatenate([dots(vectors + [w], w), cross]), BOTH) / nparam  40 us
    psum x1, blocking collectives, shards(): lax.psum(jnp.concatenate([dots(vectors + [w], w)] + gram_rows), BOTH)  39.6 us
    unnamed x9, local copies, waits for them, and re-layouts  25.7 us
    dot_general x2, matrix products, hessian(): part = jnp.dot(activations.T, scaled, preferred_element_type=jnp.float32)  23.4 us
  transfers between devices with their start and end apart: 8, of which 7 were waited for; matrix products, arithmetic and copies ran while one was open for 21% of the time, Pallas kernels for 0%

profile of v2, /device:TPU:0, one launch (start us, length us, event | category | flops | bytes accessed | tf_op | source)
XLA Modules:
  0.0 595.6 jit_solution(14398438793165796609)
XLA Ops:
  7.2 0.7 all-gather.9.cloned.1.call-update
  7.9 2.5 multiply_reduce_fusion.5
  10.4 42.6 %psum.28 = f32[]{:T(128)} all-reduce(f32[]{:T(128)} %multiply_reduce_fusion.5), channel_id=1, replica_groups=mesh['dp'=8,'tensor'=4] {'dp','tensor'}, use_global_device_ids=true, to_apply=%region_1.0 | all-reduce | flops 1 | bytes 8 | tf_op jit(solution)/shard_map/psum | solution.py:38
  53.7 1.5 broadcast_divide_fusion
  55.2 4.9 all-gather.9.cloned.1.call-done
  60.1 1.0 convert_element_type.53
  61.2 4.4 copy.45
  65.6 13.5 %fusion.26 = f32[1024,1280]{0,1:T(8,128)} fusion(bf16[1024,1280]{0,1:T(8,128)(2,1)} %copy.45, bf16[2560,1280]{1,0:T(8,128)(2,1)} %all-gather.9.cloned.1.call-done, bf16[1024,2560]{1,0:T(8,128)(2,1)} %param.5), kind=kOutput, calls=%fused_computation.48 | convolution fusion | flops 6713507840 | bytes 19660800 | tf_op jit(solution)/shard_map/dot_general | solution.py:43
  79.1 29.5 %all-gather.11.cloned.1.call-done = bf16[2560,1280]{1,0:T(8,128)(2,1)} async-done(((bf16[320,1280]{1,0:T(8,128)(2,1)}), bf16[2560,1280]{1,0:T(8,128)(2,1)}) %all-gather.11.cloned.1.call-update) | async-done | bytes 6553616 | tf_op jit(solution)/shard_map/all_gather | solution.py:53
  108.6 10.8 %fusion.50 = f32[1280,1024]{1,0:T(8,128)S(1)} fusion(bf16[2560,1280]{1,0:T(8,128)(2,1)} %all-gather.11.cloned.1.call-done, bf16[1024,2560]{1,0:T(8,128)(2,1)} %param.5), kind=kOutput, calls=%fused_computation.91 | convolution fusion | flops 6710886400 | bytes 17039360 | tf_op jit(solution)/shard_map/dot_general | solution.py:56
  119.4 2.3 copy-done.2
  121.8 11.3 %fusion.3 = bf16[2560,1280]{0,1:T(8,128)(2,1)} fusion(bf16[1024,2560]{1,0:T(8,128)(2,1)} %param.5, f32[1280,1024]{1,0:T(8,128)S(1)} %fusion.50, f32[1024,1280]{0,1:T(8,128)S(1)} %copy-done.1), kind=kOutput, calls=%fused_computation.16 | convolution fusion | flops 6720716800 | bytes 22282240 | tf_op jit(solution)/shard_map/dot_general | solution.py:61
  133.1 9.5 %copy.56 = bf16[2560,1280]{1,0:T(8,128)(2,1)} copy(bf16[2560,1280]{0,1:T(8,128)(2,1)} %fusion.3) | data formatting | bytes 13107200
  142.6 3.2 convert_element_type.51
  145.8 1.9 fusion.45
  148.0 3.8 slice_bitcast_fusion.3
  151.8 7.7 %multiply_reduce_fusion = (f32[5]{0:T(128)S(1)}, f32[5]{0:T(128)S(1)}, f32[5]{0:T(128)S(1)}, f32[5]{0:T(128)S(1)}, f32[5]{0:T(128)S(1)}) fusion(f32[320,1280]{1,0:T(8,128)S(1)} %broadcast_divide_fusion, f32[1,320,1280]{2,1,0:T(8,128)S(1)} %bitcast.124, f32[4,320,1280]{2,1,0:T(8,128)} %param.9, f32[320,1280]{1,0:T(8,128)S(1)} %get-tuple-element.30, ...), kind=kLoop, calls=%fused_computation.19 | loop fusion | flops 22527976 | bytes 16384100 | tf_op jit(solution)/shard_map/reduce_sum | solution.py:13
  159.5 46.2 %reduce-scatter.7.cloned.1.call-done = bf16[320,1280]{1,0:T(8,128)(2,1)} async-done(((bf16[2560,1280]{1,0:T(8,128)(2,1)}), bf16[320,1280]{1,0:T(8,128)(2,1)}) %reduce-scatter.7.cloned.1.call-update) | async-done | bytes 819216 | tf_op jit(solution)/shard_map/reduce_scatter | solution.py:62
  205.8 1.4 fusion.47
  207.1 3.6 fusion.1
  210.8 39.6 %psum.29 = f32[31]{0:T(128)S(1)} all-reduce(f32[31]{0:T(128)S(1)} %concatenate.18), channel_id=1, replica_groups=mesh['dp'=8,'tensor'=4] {'dp','tensor'}, use_global_device_ids=true, to_apply=%region_9.0 | all-reduce | flops 31 | bytes 248 | tf_op jit(solution)/shard_map/psum | solution.py:76
  253.2 0.7 multiply_reduce_fusion.8
  254.5 0.6 fusion.49
  255.2 6.9 %subtract_divide_fusion.1 = f32[320,1280]{1,0:T(8,128)S(1)} fusion(f32[320,1280]{1,0:T(8,128)S(1)} %broadcast_divide_fusion, f32[]{:T(128)} %sqrt.10, f32[]{:T(128)} %bitcast.13, f32[]{:T(128)} %bitcast.12, f32[]{:T(128)} %bitcast.11, f32[]{:T(128)} %bitcast.10, f32[]{:T(128)} %bitcast.9, bf16[320,1280]{1,0:T(8,128)(2,1)} %reduce-scatter.7.cloned.1.call-done, ...), kind=kLoop, calls=%fused_computation.56 | loop fusion | flops 4915200 | bytes 10649624 | tf_op jit(solution)/shard_map/div | solution.py:26
  262.1 21.3 %all-gather.7.cloned.1.call-done = bf16[2,2560,1280]{2,1,0:T(8,128)(2,1)} async-done(((bf16[2,320,1280]{2,1,0:T(8,128)(2,1)}), bf16[2,2560,1280]{2,1,0:T(8,128)(2,1)}) %all-gather.7.cloned.1.call-update) | async-done | bytes 13107216 | tf_op jit(solution)/shard_map/all_gather | solution.py:53
  283.4 1.0 convert_element_type.58
  284.4 48.1 %all-gather.15.cloned.1.call-done = bf16[2560,1280]{1,0:T(8,128)(2,1)} async-done(((bf16[320,1280]{1,0:T(8,128)(2,1)}), bf16[2560,1280]{1,0:T(8,128)(2,1)}) %all-gather.15.cloned.1.call-update) | async-done | bytes 6553616 | tf_op jit(solution)/shard_map/all_gather | solution.py:53
  332.5 16.5 %fusion.22 = (f32[1024]{0:T(1024)S(1)}, f32[1024]{0:T(1024)S(1)}, bf16[1024,1280]{0,1:T(8,128)(2,1)}, f32[1280,1024]{1,0:T(8,128)S(1)}) fusion(f32[1280,1024]{1,0:T(8,128)} %copy-done.2, f32[1024,1280]{0,1:T(8,128)} %fusion.26, bf16[2560,1280]{1,0:T(8,128)(2,1)} %all-gather.15.cloned.1.call-done, bf16[1024,2560]{1,0:T(8,128)(2,1)} %param.5), kind=kOutput, calls=%fused_computation.41 | convolution fusion | flops 6718748672 | bytes 30154752 | tf_op jit(solution)/shard_map/dot_general | solution.py:56
  349.0 12.1 %fusion.4 = bf16[2560,1280]{0,1:T(8,128)(2,1)} fusion(bf16[1024,2560]{1,0:T(8,128)(2,1)} %param.5, f32[1280,1024]{1,0:T(8,128)S(1)} %get-tuple-element.55, f32[1024,1280]{0,1:T(8,128)} %fusion.26), kind=kOutput, calls=%fused_computation.17 | convolution fusion | flops 6720716800 | bytes 22282240 | tf_op jit(solution)/shard_map/dot_general | solution.py:61
  361.1 9.5 %copy.58 = bf16[2560,1280]{1,0:T(8,128)(2,1)} copy(bf16[2560,1280]{0,1:T(8,128)(2,1)} %fusion.4) | data formatting | bytes 13107200
  370.7 0.7 all-gather.13.cloned.1.call-update
  371.5 3.6 fusion.2
  375.0 58.8 %reduce-scatter.9.cloned.1.call-done = bf16[320,1280]{1,0:T(8,128)(2,1)} async-done(((bf16[2560,1280]{1,0:T(8,128)(2,1)}), bf16[320,1280]{1,0:T(8,128)(2,1)}) %reduce-scatter.9.cloned.1.call-update) | async-done | bytes 819216 | tf_op jit(solution)/shard_map/reduce_scatter | solution.py:62
  433.8 1.4 fusion.46
  435.2 4.6 fusion
  439.9 40.0 %psum.30 = f32[13]{0:T(128)S(1)} all-reduce(f32[13]{0:T(128)S(1)} %pad_maximum_fusion.4), channel_id=1, replica_groups=mesh['dp'=8,'tensor'=4] {'dp','tensor'}, use_global_device_ids=true, to_apply=%region_16.0 | all-reduce | flops 13 | bytes 104 | tf_op jit(solution)/shard_map/psum | solution.py:87
  482.8 0.7 multiply_reduce_fusion.6
  484.2 0.7 fusion.48
  484.9 9.0 %subtract_divide_fusion = f32[320,1280]{1,0:T(8,128)} fusion(f32[320,1280]{1,0:T(8,128)S(1)} %subtract_divide_fusion.1, f32[320,1280]{1,0:T(8,128)S(1)} %broadcast_divide_fusion, f32[]{:T(128)} %sqrt.11, f32[]{:T(128)} %bitcast.26, f32[]{:T(128)} %bitcast.25, f32[]{:T(128)} %bitcast.24, f32[]{:T(128)} %bitcast.23, f32[]{:T(128)} %bitcast.22, f32[]{:T(128)} %bitcast.21, ...), kind=kLoop, calls=%fused_computation.55 | loop fusion | flops 5734400 | bytes 12288028 | tf_op jit(solution)/shard_map/div | solution.py:26
  493.9 17.2 %all-gather.13.cloned.1.call-done = bf16[2,2560,1280]{2,1,0:T(8,128)(2,1)} async-done(((bf16[2,320,1280]{2,1,0:T(8,128)(2,1)}), bf16[2,2560,1280]{2,1,0:T(8,128)(2,1)}) %all-gather.13.cloned.1.call-update) | async-done | bytes 13107216 | tf_op jit(solution)/shard_map/all_gather | solution.py:53
  511.0 2.4 convert_element_type.65
  514.1 11.3 %fusion.18 = f32[1024]{0:T(1024)S(1)} fusion(bf16[1024,1280]{0,1:T(8,128)(2,1)} %get-tuple-element.27, bf16[1024,2560]{1,0:T(8,128)(2,1)} %param.5, bf16[2,2560,1280]{2,1,0:T(8,128)(2,1)} %all-gather.7.cloned.1.call-done), kind=kOutput, calls=%fused_computation.37 | convolution fusion | flops 6714817536 | bytes 14422016 | tf_op jit(solution)/shard_map/dot_general | solution.py:56
  525.6 11.3 %fusion.17 = f32[1024]{0:T(1024)S(1)} fusion(bf16[1024,1280]{0,1:T(8,128)(2,1)} %get-tuple-element.27, bf16[1024,2560]{1,0:T(8,128)(2,1)} %param.5, bf16[2,2560,1280]{2,1,0:T(8,128)(2,1)} %all-gather.7.cloned.1.call-done), kind=kOutput, calls=%fused_computation.36 | convolution fusion | flops 6714817536 | bytes 14422016 | tf_op jit(solution)/shard_map/dot_general | solution.py:56
  537.6 12.5 %fusion.20 = f32[1024]{0:T(1024)S(1)} fusion(bf16[1024,1280]{0,1:T(8,128)(2,1)} %get-tuple-element.27, bf16[1024,2560]{1,0:T(8,128)(2,1)} %param.5, bf16[2,2560,1280]{2,1,0:T(8,128)(2,1)} %all-gather.13.cloned.1.call-done), kind=kOutput, calls=%fused_computation.39 | convolution fusion | flops 6714817536 | bytes 14422016 | tf_op jit(solution)/shard_map/dot_general | solution.py:56
  550.4 11.5 %fusion.19 = f32[1024]{0:T(1024)S(1)} fusion(bf16[1024,1280]{0,1:T(8,128)(2,1)} %get-tuple-element.27, bf16[1024,2560]{1,0:T(8,128)(2,1)} %param.5, bf16[2,2560,1280]{2,1,0:T(8,128)(2,1)} %all-gather.13.cloned.1.call-done), kind=kOutput, calls=%fused_computation.38 | convolution fusion | flops 6714817536 | bytes 14422016 | tf_op jit(solution)/shard_map/dot_general | solution.py:56
  562.7 1.9 pad_maximum_fusion.2
  564.6 11.3 %fusion.23 = f32[1024]{0:T(1024)S(1)} fusion(bf16[1024,1280]{0,1:T(8,128)(2,1)} %get-tuple-element.27, bf16[2560,1280]{1,0:T(8,128)(2,1)} %all-gather.17.cloned.1.call-done, bf16[1024,2560]{1,0:T(8,128)(2,1)} %param.5), kind=kOutput, calls=%fused_computation.42 | convolution fusion | flops 6714817536 | bytes 14422016 | tf_op jit(solution)/shard_map/dot_general | solution.py:56
  576.3 11.7 %psum.31 = f32[2,7]{1,0:T(2,128)S(1)} all-reduce(f32[2,7]{1,0:T(2,128)S(1)} %stack.88), channel_id=1, replica_groups=mesh['dp'=8,'tensor'=4] {'tensor'}, use_global_device_ids=true, to_apply=%region_34.35 | all-reduce | flops 14 | bytes 112 | tf_op jit(solution)/shard_map/psum | solution.py:98
  (60 shorter events, 7.3 us)
Async XLA Ops:
  7.2 53.0 %all-gather.9.cloned.1.call-start = ((), (), s32[]{:S(2)}) async-start(), calls=%async_computation.3 | async-start | bytes 7372800 | tf_op jit(solution)/shard_map/all_gather | solution.py:41
  7.9 100.7 %all-gather.11.cloned.1.call-start = ((), (), s32[]{:S(2)}) async-start(), calls=%async_computation.4 | async-start | bytes 7372800 | tf_op jit(solution)/shard_map/all_gather | solution.py:53
  61.2 144.6 %reduce-scatter.7.cloned.1.call-start = ((), (), s32[]{:S(2)}) async-start(), calls=%async_computation.8 | async-start | bytes 7372800 | tf_op jit(solution)/shard_map/reduce_scatter | solution.py:62
  108.6 13.2 %copy-start.1 = (f32[1024,1280]{0,1:T(8,128)S(1)}, f32[1024,1280]{0,1:T(8,128)}, u32[]{:S(2)}) copy-start(f32[1024,1280]{0,1:T(8,128)} %fusion.26) | copy-start | bytes 15728644
  119.4 2.4 copy-start.2
  142.6 140.8 %all-gather.7.cloned.1.call-start = ((), (), s32[]{:S(2)}) async-start(), calls=%async_computation.2 | async-start | bytes 14745600 | tf_op jit(solution)/shard_map/all_gather | solution.py:53
  147.8 184.8 %all-gather.15.cloned.1.call-start = ((), (), s32[]{:S(2)}) async-start(), calls=%async_computation.6 | async-start | bytes 7372800 | tf_op jit(solution)/shard_map/all_gather | solution.py:53
  284.4 149.4 %reduce-scatter.9.cloned.1.call-start = ((), (), s32[]{:S(2)}) async-start(), calls=%async_computation.9 | async-start | bytes 7372800 | tf_op jit(solution)/shard_map/reduce_scatter | solution.py:62
  370.7 140.4 %all-gather.13.cloned.1.call-start = ((), (), s32[]{:S(2)}) async-start(), calls=%async_computation.5 | async-start | bytes 14745600 | tf_op jit(solution)/shard_map/all_gather | solution.py:53
  371.4 193.2 %all-gather.17.cloned.1.call-start = ((), (), s32[]{:S(2)}) async-start(), calls=%async_computation.7 | async-start | bytes 7372800 | tf_op jit(solution)/shard_map/all_gather | solution.py:53
  550.4 12.3 %copy-start = (f32[320,1280]{1,0:T(8,128)S(1)}, f32[320,1280]{1,0:T(8,128)}, u32[]{:S(2)}) copy-start(f32[320,1280]{1,0:T(8,128)} %subtract_divide_fusion) | copy-start | bytes 4915204
Sparse Core Ops, SparseCore 0:
  9.9 50.1 all-gather.8
  62.0 46.5 all-gather.10
  142.7 62.9 reduce-scatter.6
  208.2 75.1 all-gather.6
  285.9 46.6 all-gather.14
  370.8 62.9 reduce-scatter.8
  435.7 75.2 all-gather.12
  513.6 46.6 all-gather.16

commit v3 on v2

--- a/solution.py
+++ b/solution.py
@@ -55,46 +55,60 @@
     def image(v):
         return jnp.dot(activations, v, preferred_element_type=jnp.float32)
 
-    def hessian(v):
-        mapped = image(gather(v.astype(jnp.bfloat16)))
+    def hessian(v, piece, ready=()):
+        full = gather(v.astype(jnp.bfloat16))
+        ready = [project(image(u)) for u in ready]
+        piece, full, ready = lax.optimization_barrier((piece, full, ready))
+        full_piece = gather(piece)
+        mapped = image(full)
         scaled = (curvature * mapped).astype(jnp.bfloat16)
         part = jnp.dot(activations.T, scaled, preferred_element_type=jnp.float32)
-        imaged = lax.psum_scatter(
-            part.astype(jnp.bfloat16), "dp", scatter_dimension=0, tiled=True
+        part, full_piece = lax.optimization_barrier(
+            (part.astype(jnp.bfloat16), full_piece)
         )
-        return imaged.astype(jnp.float32), project(mapped)
+        imaged = lax.psum_scatter(part, "dp", scatter_dimension=0, tiled=True)
+        return imaged, project(mapped), full_piece, ready
+
+    def reduce_beside(local, done):
+        local, done = lax.optimization_barrier((local, done))
+        return lax.psum(local, BOTH) / nparam, done
 
     vectors = [stored[k] for k in range(ks)] + [q0]
     table = stored.astype(jnp.bfloat16)
-    half = ks // 2
+    cuts = [1, ks - 1]
+    n = ks + 1
+    m = n + 1
 
-    w, proj_q0 = hessian(q0)
-    n = ks + 1
-    table_a, _ = lax.optimization_barrier((table[:half], w[0, 0]))
+    w, proj_q0, piece, _ = hessian(q0, table[: cuts[0]])
+    table_a, _ = lax.optimization_barrier((table[cuts[0] : cuts[1]], w[0, 0]))
     full_a = gather(table_a)
+    done = [project(image(v)) for v in piece]
+    w = w.astype(jnp.float32)
     gram_rows = [dots(vectors, v) for v in vectors]
-    sums = lax.psum(jnp.concatenate([dots(vectors + [w], w)] + gram_rows), BOTH) / nparam
+    sums, done = reduce_beside(jnp.concatenate([dots(vectors + [w], w)] + gram_rows), done)
     gram = sums[n + 1 :].reshape(n, n)
     q1, coef_first = orthogonalize(vectors, w, sums[:n], sums[n], gram)
 
     full_a, q1 = lax.optimization_barrier((full_a, q1))
     vectors = vectors + [q1]
-    w, proj_q1 = hessian(q1)
+    w_sent, proj_q1, piece, ready = hessian(q1, table[cuts[1] :], full_a)
     cross = dots(vectors, q1)
-    m = n + 1
-    table_b, _ = lax.optimization_barrier((table[half:], w[0, 0]))
-    full_b = gather(table_b)
-    sums = lax.psum(jnp.concatenate([dots(vectors + [w], w), cross]), BOTH) / nparam
+    done = done + list(ready) + [project(image(v)) for v in piece]
+    w_sent, done, cross = lax.optimization_barrier((w_sent, done, cross))
+    full_w = gather(w_sent)
+    w = w_sent.astype(jnp.float32)
+    sums, done = reduce_beside(jnp.concatenate([dots(vectors + [w], w), cross]), done)
     cross = sums[m + 1 :]
     gram = jnp.concatenate(
         [jnp.concatenate([gram, cross[:n, None]], axis=1), cross[None, :]], axis=0
     )
     q2, coef_second = orthogonalize(vectors, w, sums[:m], sums[m], gram)
-    full_b, q2 = lax.optimization_barrier((full_b, q2))
 
-    parts = [project(image(full_a[k])) for k in range(half)]
-    parts += [project(image(full_b[k])) for k in range(ks - half)]
-    parts += [proj_q0, proj_q1, project(image(gather(q2.astype(jnp.bfloat16))))]
+    parts = done + [proj_q0, proj_q1]
+    last = project(image(full_w))
+    for k in range(m):
+        last = last - coef_second[k] * parts[k]
+    parts = parts + [last / coef_second[m]]
     projections = lax.psum(jnp.stack(parts, axis=1), "tensor")
     projections = projections / math.sqrt(float(tok_ex) * nparam)
     return (jnp.stack([q1, q2]), coef_first, coef_second, projections)

time: 606 us -> 588 us (0.970)
  waiting for transfers between devices: 227 us -> 210 us
  matrix products: 122 us -> 112 us
  local copies, waits for them, and re-layouts: 35.2 us -> 43.8 us
    reduce_scatter x2 -> x1, waiting for transfers between devices: 105 us -> 39.1 us  [hessian(): imaged = lax.psum_scatter(part, 'dp', scatter_dimension=0, tiled=True)]
    unnamed x8 -> x10, waiting for transfers between devices: 1.47 us -> 48.5 us
    div x2 -> x1, other arithmetic: 15.9 us -> 6.98 us  [orthogonalize(): return (remainder / norm, jnp.concatenate([total, norm[None]]))]
    another operation x1 -> x2, other arithmetic: 1.92 us -> 9.77 us  [shards(): return (jnp.stack([q1, q2]), coef_first, coef_second, projections)]
    dot_general x7, matrix products: 85.3 us -> 78.4 us  [image(): return jnp.dot(activations, v, preferred_element_type=jnp.float32)]
    unnamed x9 -> x25, local copies, waits for them, and re-layouts: 25.7 us -> 27.6 us
    all_gather x5 -> x6, waiting for transfers between devices: 116 us -> 117 us  [gather(): return lax.all_gather(v, 'dp', axis=v.ndim - 2, tiled=True)]
  transfers between devices with their start and end apart: 8 -> 9, of which waited for: 7 -> 8; matrix products, arithmetic and copies ran while one was open for 21% -> 29% of each run, Pallas kernels for 0% -> 0%
where the time goes in v3:
time: 588 us; the launch traced here: 578 us
  waiting for transfers between devices  210 us (36%)
  blocking collectives  133 us (23%)
  matrix products  112 us (19%)
  other arithmetic  59.1 us (10%)
  local copies, waits for them, and re-layouts  43.8 us (7%)
  between operations  19 us (3%)
    all_gather x6, waiting for transfers between devices, gather(): return lax.all_gather(v, 'dp', axis=v.ndim - 2, tiled=True)  117 us
    psum x2, blocking collectives, reduce_beside(): return (lax.psum(local, BOTH) / nparam, done)  79.3 us
    dot_general x7, matrix products, image(): return jnp.dot(activations, v, preferred_element_type=jnp.float32)  78.4 us
    unnamed x10, waiting for transfers between devices  48.5 us
    psum x1, blocking collectives, shards(): square_sum = lax.psum(jnp.sum(start_vector * start_vector), BOTH) / nparam  42.6 us
    reduce_scatter x1, waiting for transfers between devices, hessian(): imaged = lax.psum_scatter(part, 'dp', scatter_dimension=0, tiled=True)  39.1 us
    unnamed x25, local copies, waits for them, and re-layouts  27.6 us
    reduce_sum x4, other arithmetic, dots(): return jnp.sum(jnp.stack(vectors) * one[None], axis=(1, 2))  21.1 us
  transfers between devices with their start and end apart: 9, of which 8 were waited for; matrix products, arithmetic and copies ran while one was open for 29% of the time, Pallas kernels for 0%

profile of v3, /device:TPU:0, one launch (start us, length us, event | category | flops | bytes accessed | tf_op | source)
XLA Modules:
  0.0 577.7 jit_solution(16215813971604091119)
XLA Ops:
  7.2 0.7 all-gather.10.cloned.1.call-update
  7.9 2.5 multiply_reduce_fusion.5
  10.4 42.6 %psum.28 = f32[]{:T(128)} all-reduce(f32[]{:T(128)} %multiply_reduce_fusion.5), channel_id=1, replica_groups=mesh['dp'=8,'tensor'=4] {'dp','tensor'}, use_global_device_ids=true, to_apply=%region_1.0 | all-reduce | flops 1 | bytes 8 | tf_op jit(solution)/shard_map/psum | solution.py:38
  53.7 1.5 broadcast_divide_fusion
  55.2 4.9 all-gather.10.cloned.1.call-done
  60.1 1.0 convert_element_type.50
  61.2 3.2 convert_element_type.48
  64.4 1.7 copy-done
  66.1 1.2 fusion.43
  67.3 41.3 %all-gather.12.cloned.1.call-done = bf16[2560,1280]{1,0:T(8,128)(2,1)} async-done(((bf16[320,1280]{1,0:T(8,128)(2,1)}), bf16[2560,1280]{1,0:T(8,128)(2,1)}) %all-gather.12.cloned.1.call-update) | async-done | bytes 6553616 | tf_op jit(solution)/shard_map/all_gather | solution.py:53
  108.7 4.6 copy.46
  113.2 12.6 %fusion.48 = (bf16[1024,1280]{0,1:T(8,128)(2,1)}, f32[1024,1280]{0,1:T(8,128)S(1)}) fusion(bf16[1024,1280]{0,1:T(8,128)(2,1)} %copy.46, bf16[2560,1280]{1,0:T(8,128)(2,1)} %all-gather.10.cloned.1.call-done, bf16[1024,2560]{1,0:T(8,128)(2,1)} %param.5), kind=kOutput, calls=%fused_computation.90 | convolution fusion | flops 6714818560 | bytes 22282240 | tf_op jit(solution)/shard_map/dot_general | solution.py:43
  125.8 11.0 %fusion.49 = f32[1280,1024]{1,0:T(8,128)S(1)} fusion(bf16[2560,1280]{1,0:T(8,128)(2,1)} %all-gather.12.cloned.1.call-done, bf16[1024,2560]{1,0:T(8,128)(2,1)S(1)} %bitcast.143), kind=kOutput, calls=%fused_computation.91 | convolution fusion | flops 6710886400 | bytes 17039360 | tf_op jit(solution)/shard_map/dot_general | solution.py:56
  136.9 2.3 copy-done.1
  139.2 8.8 %fusion.3 = bf16[2560,1280]{0,1:T(8,128)(2,1)} fusion(bf16[1024,2560]{1,0:T(8,128)(2,1)S(1)} %bitcast.143, f32[1280,1024]{1,0:T(8,128)S(1)} %fusion.49, f32[1024,1280]{0,1:T(8,128)S(1)} %get-tuple-element.97), kind=kOutput, calls=%fused_computation.16 | convolution fusion | flops 6720716800 | bytes 22282240 | tf_op jit(solution)/shard_map/dot_general | solution.py:65
  148.0 9.2 %all-gather.14.cloned.1.call-done = bf16[1,2560,1280]{2,1,0:T(8,128)(2,1)} async-done(((bf16[1,320,1280]{2,1,0:T(8,128)(2,1)}), bf16[1,2560,1280]{2,1,0:T(8,128)(2,1)}) %all-gather.14.cloned.1.call-update) | async-done | bytes 6553616 | tf_op jit(solution)/shard_map/all_gather | solution.py:53
  157.1 9.6 %copy.58 = bf16[2560,1280]{1,0:T(8,128)(2,1)} copy(bf16[2560,1280]{0,1:T(8,128)(2,1)} %fusion.3) | data formatting | bytes 13107200
  166.8 2.7 slice.112
  169.8 4.1 slice_bitcast_fusion.3
  174.0 9.2 %multiply_reduce_fusion = (f32[5]{0:T(128)S(1)}, f32[5]{0:T(128)S(1)}, f32[5]{0:T(128)S(1)}, f32[5]{0:T(128)S(1)}, f32[5]{0:T(128)S(1)}) fusion(f32[320,1280]{1,0:T(8,128)S(1)} %broadcast_divide_fusion, f32[1,320,1280]{2,1,0:T(8,128)S(1)} %bitcast.126, f32[4,320,1280]{2,1,0:T(8,128)} %param.9, f32[320,1280]{1,0:T(8,128)S(1)} %get-tuple-element.71, ...), kind=kLoop, calls=%fused_computation.19 | loop fusion | flops 22527976 | bytes 16384100 | tf_op jit(solution)/shard_map/reduce_sum | solution.py:13
  183.2 7.4 %fusion.15 = f32[1024]{0:T(1024)S(1)} fusion(bf16[1024,1280]{0,1:T(8,128)(2,1)S(1)} %copy-done.3, bf16[1024,2560]{1,0:T(8,128)(2,1)S(1)} %bitcast.145, bf16[1,2560,1280]{2,1,0:T(8,128)(2,1)S(1)} %bitcast.141), kind=kOutput, calls=%fused_computation.34 | convolution fusion | flops 6714817536 | bytes 14422016 | tf_op jit(solution)/shard_map/dot_general | solution.py:56
  190.8 39.1 %reduce-scatter.7.cloned.1.call-done = bf16[320,1280]{1,0:T(8,128)(2,1)} async-done(((bf16[2560,1280]{1,0:T(8,128)(2,1)}), bf16[320,1280]{1,0:T(8,128)(2,1)}) %reduce-scatter.7.cloned.1.call-update) | async-done | bytes 819216 | tf_op jit(solution)/shard_map/reduce_scatter | solution.py:69
  229.9 1.4 fusion.45
  231.2 3.6 fusion.1
  234.9 39.7 %psum.29 = f32[31]{0:T(128)S(1)} all-reduce(f32[31]{0:T(128)S(1)} %concatenate.18), channel_id=1, replica_groups=mesh['dp'=8,'tensor'=4] {'dp','tensor'}, use_global_device_ids=true, to_apply=%region_11.0 | all-reduce | flops 31 | bytes 248 | tf_op jit(solution)/shard_map/psum | solution.py:74
  279.3 7.0 %subtract_divide_fusion = f32[320,1280]{1,0:T(8,128)S(1)} fusion(f32[320,1280]{1,0:T(8,128)S(1)} %broadcast_divide_fusion, f32[]{:T(128)} %sqrt.10, f32[]{:T(128)} %bitcast.15, f32[]{:T(128)} %bitcast.14, f32[]{:T(128)} %bitcast.13, f32[]{:T(128)} %bitcast.12, f32[]{:T(128)} %bitcast.11, bf16[320,1280]{1,0:T(8,128)(2,1)} %reduce-scatter.7.cloned.1.call-done, ...), kind=kLoop, calls=%fused_computation.54 | loop fusion | flops 4915200 | bytes 10649624 | tf_op jit(solution)/shard_map/div | solution.py:26
  286.3 20.7 %all-gather.8.cloned.1.call-done = bf16[2,2560,1280]{2,1,0:T(8,128)(2,1)} async-done(((bf16[2,320,1280]{2,1,0:T(8,128)(2,1)}), bf16[2,2560,1280]{2,1,0:T(8,128)(2,1)}) %all-gather.8.cloned.1.call-update) | async-done | bytes 13107216 | tf_op jit(solution)/shard_map/all_gather | solution.py:53
  307.0 1.0 convert_element_type.57
  308.3 11.3 %fusion.17 = f32[1024]{0:T(1024)S(1)} fusion(bf16[1024,1280]{0,1:T(8,128)(2,1)} %get-tuple-element.96, bf16[1024,2560]{1,0:T(8,128)(2,1)} %param.5, bf16[2,2560,1280]{2,1,0:T(8,128)(2,1)} %all-gather.8.cloned.1.call-done), kind=kOutput, calls=%fused_computation.36 | convolution fusion | flops 6714817536 | bytes 14422016 | tf_op jit(solution)/shard_map/dot_general | solution.py:56
  319.8 11.3 %fusion.16 = f32[1024]{0:T(1024)S(1)} fusion(bf16[1024,1280]{0,1:T(8,128)(2,1)} %get-tuple-element.96, bf16[1024,2560]{1,0:T(8,128)(2,1)} %param.5, bf16[2,2560,1280]{2,1,0:T(8,128)(2,1)} %all-gather.8.cloned.1.call-done), kind=kOutput, calls=%fused_computation.35 | convolution fusion | flops 6714817536 | bytes 14422016 | tf_op jit(solution)/shard_map/dot_general | solution.py:56
  331.3 24.8 %all-gather.16.cloned.1.call-done = bf16[2560,1280]{1,0:T(8,128)(2,1)} async-done(((bf16[320,1280]{1,0:T(8,128)(2,1)}), bf16[2560,1280]{1,0:T(8,128)(2,1)}) %all-gather.16.cloned.1.call-update) | async-done | bytes 6553616 | tf_op jit(solution)/shard_map/all_gather | solution.py:53
  356.6 14.6 %fusion.20 = (f32[1024]{0:T(1024)S(1)}, f32[1024]{0:T(1024)S(1)}, f32[1280,1024]{1,0:T(8,128)S(1)}) fusion(bf16[1024,1280]{0,1:T(8,128)(2,1)} %get-tuple-element.96, f32[1280,1024]{1,0:T(8,128)} %copy-done.1, bf16[2560,1280]{1,0:T(8,128)(2,1)} %all-gather.16.cloned.1.call-done, bf16[1024,2560]{1,0:T(8,128)(2,1)} %param.5), kind=kOutput, calls=%fused_computation.39 | convolution fusion | flops 6717437952 | bytes 24911872 | tf_op jit(solution)/shard_map/dot_general | solution.py:56
  371.2 12.3 %fusion.4 = bf16[2560,1280]{0,1:T(8,128)(2,1)} fusion(bf16[1024,2560]{1,0:T(8,128)(2,1)} %param.5, f32[1280,1024]{1,0:T(8,128)S(1)} %get-tuple-element.98, f32[1024,1280]{0,1:T(8,128)} %copy-done.2), kind=kOutput, calls=%fused_computation.17 | convolution fusion | flops 6720716800 | bytes 22282240 | tf_op jit(solution)/shard_map/dot_general | solution.py:65
  383.5 21.3 %all-gather.18.cloned.1.call-done = bf16[1,2560,1280]{2,1,0:T(8,128)(2,1)} async-done(((bf16[1,320,1280]{2,1,0:T(8,128)(2,1)}), bf16[1,2560,1280]{2,1,0:T(8,128)(2,1)}) %all-gather.18.cloned.1.call-update) | async-done | bytes 6553616 | tf_op jit(solution)/shard_map/all_gather | solution.py:53
  404.8 9.5 %copy.60 = bf16[2560,1280]{1,0:T(8,128)(2,1)} copy(bf16[2560,1280]{0,1:T(8,128)(2,1)} %fusion.4) | data formatting | bytes 13107200
  414.5 3.7 fusion.2
  418.2 11.3 %fusion.18 = f32[1024]{0:T(1024)S(1)} fusion(bf16[1024,1280]{0,1:T(8,128)(2,1)S(1)} %copy-done.4, bf16[1024,2560]{1,0:T(8,128)(2,1)} %param.5, bf16[1,2560,1280]{2,1,0:T(8,128)(2,1)} %all-gather.18.cloned.1.call-done), kind=kOutput, calls=%fused_computation.37 | convolution fusion | flops 6714817536 | bytes 14422016 | tf_op jit(solution)/shard_map/dot_general | solution.py:56
  429.7 47.7 %reduce-scatter.9.cloned.1.call-done = bf16[320,1280]{1,0:T(8,128)(2,1)} async-done(((bf16[2560,1280]{1,0:T(8,128)(2,1)}), bf16[320,1280]{1,0:T(8,128)(2,1)}) %reduce-scatter.9.cloned.1.call-update) | async-done | bytes 819216
  477.4 2.2 copy.61
  479.6 2.2 copy.48
  482.9 1.4 fusion.44
  484.3 4.6 fusion
  489.0 39.7 %psum.30 = f32[13]{0:T(128)S(1)} all-reduce(f32[13]{0:T(128)S(1)} %pad_maximum_fusion.4), channel_id=1, replica_groups=mesh['dp'=8,'tensor'=4] {'dp','tensor'}, use_global_device_ids=true, to_apply=%region_24.0 | all-reduce | flops 13 | bytes 104 | tf_op jit(solution)/shard_map/psum | solution.py:74
  534.6 7.7 %divide_bitcast_fusion = f32[1,320,1280]{2,1,0:T(8,128)S(1)} fusion(f32[320,1280]{1,0:T(8,128)S(1)} %subtract_divide_fusion, f32[320,1280]{1,0:T(8,128)S(1)} %broadcast_divide_fusion, f32[]{:T(128)} %sqrt.11, f32[]{:T(128)} %bitcast.34, f32[]{:T(128)} %bitcast.33, f32[]{:T(128)} %bitcast.32, f32[]{:T(128)} %bitcast.31, f32[]{:T(128)} %bitcast.30, ...), kind=kLoop, calls=%fused_computation.53 | loop fusion | flops 5734400 | bytes 12288028 | tf_op jit(solution)/shard_map/stack | solution.py:114
  542.3 2.1 pad_maximum_fusion.2
  544.3 11.3 %fusion.21 = f32[1024]{0:T(1024)S(1)} fusion(bf16[1024,1280]{0,1:T(8,128)(2,1)} %get-tuple-element.96, bf16[2560,1280]{1,0:T(8,128)(2,1)} %all-gather.20.cloned.1.call-done, bf16[1024,2560]{1,0:T(8,128)(2,1)} %param.5), kind=kOutput, calls=%fused_computation.40 | convolution fusion | flops 6714817536 | bytes 14422016 | tf_op jit(solution)/shard_map/dot_general | solution.py:56
  555.8 3.8 divide_bitcast_fusion.1
  559.8 10.6 %psum.31 = f32[2,7]{1,0:T(2,128)S(1)} all-reduce(f32[2,7]{1,0:T(2,128)S(1)} %stack.88), channel_id=1, replica_groups=mesh['dp'=8,'tensor'=4] {'tensor'}, use_global_device_ids=true, to_apply=%region_34.35 | all-reduce | flops 14 | bytes 112 | tf_op jit(solution)/shard_map/psum | solution.py:112
  (85 shorter events, 10.9 us)
Async XLA Ops:
  7.2 53.0 %all-gather.10.cloned.1.call-start = ((), (), s32[]{:S(2)}) async-start(), calls=%async_computation.3 | async-start | bytes 7372800 | tf_op jit(solution)/shard_map/all_gather | solution.py:41
  7.9 100.7 %all-gather.12.cloned.1.call-start = ((), (), s32[]{:S(2)}) async-start(), calls=%async_computation.4 | async-start | bytes 7372800 | tf_op jit(solution)/shard_map/all_gather | solution.py:53
  61.1 96.0 %all-gather.14.cloned.1.call-start = ((), (), s32[]{:S(2)}) async-start(), calls=%async_computation.5 | async-start | bytes 7372800 | tf_op jit(solution)/shard_map/all_gather | solution.py:53
  64.4 1.7 copy-start
  108.6 121.3 %reduce-scatter.7.cloned.1.call-start = ((), (), s32[]{:S(2)}) async-start(), calls=%async_computation.9 | async-start | bytes 7372800 | tf_op jit(solution)/shard_map/reduce_scatter | solution.py:69
  108.7 17.1 %slice-start.2 = ((s8[5242880]{0:T(1024)(128)(4,1)}), s8[1048576]{0:T(1024)(128)(4,1)S(1)}, s32[]{:S(2)}) async-start(s8[5242880]{0:T(1024)(128)(4,1)} %bitcast.142), calls=%async_computation.13 | async-start | bytes 2097152
  113.2 12.6 %slice-start.3 = ((s8[5242880]{0:T(1024)(128)(4,1)}), s8[4194304]{0:T(1024)(128)(4,1)S(1)}, s32[]{:S(2)}) async-start(s8[5242880]{0:T(1024)(128)(4,1)} %bitcast.142), calls=%async_computation.14 | async-start | bytes 8388608
  125.8 11.1 %copy-start.2 = (f32[1024,1280]{0,1:T(8,128)}, f32[1024,1280]{0,1:T(8,128)S(1)}, u32[]{:S(2)}) copy-start(f32[1024,1280]{0,1:T(8,128)S(1)} %get-tuple-element.97) | copy-start | bytes 15728644
  136.9 2.3 copy-start.1
  166.7 140.3 %all-gather.8.cloned.1.call-start = ((), (), s32[]{:S(2)}) async-start(), calls=%async_computation.2 | async-start | bytes 14745600 | tf_op jit(solution)/shard_map/all_gather | solution.py:53
  169.5 186.5 %all-gather.16.cloned.1.call-start = ((), (), s32[]{:S(2)}) async-start(), calls=%async_computation.6 | async-start | bytes 7372800 | tf_op jit(solution)/shard_map/all_gather | solution.py:53
  169.8 13.4 %slice-start = ((s8[6553600]{0:T(1024)(128)(4,1)}), s8[4194304]{0:T(1024)(128)(4,1)S(1)}, s32[]{:S(2)}) async-start(s8[6553600]{0:T(1024)(128)(4,1)} %bitcast.140), calls=%async_computation.11 | async-start | bytes 8388608
  169.8 13.4 %slice-start.4 = ((s8[5242880]{0:T(1024)(128)(4,1)}), s8[4194304]{0:T(1024)(128)(4,1)S(1)}, s32[]{:S(2)}) async-start(s8[5242880]{0:T(1024)(128)(4,1)} %bitcast.144), calls=%async_computation.15 | async-start | bytes 8388608
  173.9 9.2 %slice-start.1 = ((s8[6553600]{0:T(1024)(128)(4,1)}), s8[2359296]{0:T(1024)(128)(4,1)S(1)}, s32[]{:S(2)}) async-start(s8[6553600]{0:T(1024)(128)(4,1)} %bitcast.140), calls=%async_computation.12 | async-start | bytes 4718592
  173.9 9.2 %slice-start.5 = ((s8[5242880]{0:T(1024)(128)(4,1)}), s8[1048576]{0:T(1024)(128)(4,1)S(1)}, s32[]{:S(2)}) async-start(s8[5242880]{0:T(1024)(128)(4,1)} %bitcast.144), calls=%async_computation.16 | async-start | bytes 2097152
  174.0 9.2 %copy-start.3 = (bf16[1024,1280]{0,1:T(8,128)(2,1)S(1)}, bf16[1024,1280]{0,1:T(8,128)(2,1)}, u32[]{:S(2)}) copy-start(bf16[1024,1280]{0,1:T(8,128)(2,1)} %get-tuple-element.96) | copy-start | bytes 7864324
  308.0 96.8 %all-gather.18.cloned.1.call-start = ((), (), s32[]{:S(2)}) async-start(), calls=%async_computation.7 | async-start | bytes 7372800 | tf_op jit(solution)/shard_map/all_gather | solution.py:53
  356.1 121.3 %reduce-scatter.9.cloned.1.call-start = ((), (), s32[]{:S(2)}) async-start(), calls=%async_computation.10 | async-start | bytes 7372800
  414.3 130.1 %all-gather.20.cloned.1.call-start = ((), (), s32[]{:S(2)}) async-start(), calls=%async_computation.8 | async-start | bytes 7372800 | tf_op jit(solution)/shard_map/all_gather | solution.py:53
  414.5 3.7 copy-start.4
Sparse Core Ops, SparseCore 0:
  9.9 50.1 all-gather.9
  62.0 46.5 all-gather.11
  110.5 46.6 all-gather.13
  166.9 62.9 reduce-scatter.6
  231.8 75.1 all-gather.7
  309.5 46.5 all-gather.15
  358.1 46.6 all-gather.17
  414.4 62.9 reduce-scatter.8
  482.0 47.8 all-gather.19
